TPU v7x, 32 devices: a whole 2x2x4 slice. The times are simulated.
32 devices in a mesh: seq: 8 (over z, core), batch: 4 (over y, x).
Axes of the slice: x: 2, y: 2, z: 4, core: 2. Of those that a mesh axis runs over, the one named last changes fastest.
Arguments:
- tokens: bfloat16 [32, 2, 512, 576], P('batch', None, 'seq'), may hold values from -6 to 6
- assign: int32 [32], P('batch'), may hold values from 0 to 31, as said below
- lengths: int32 [32], replicated, may hold values from 128 to 1024, as said below
- gain_attn: bfloat16 [576], replicated, may hold values from 0.5 to 1.5
- query_weight: bfloat16 [576, 576], replicated, may hold values from -0.25 to 0.25
- key_weight: bfloat16 [576, 192], replicated, may hold values from -0.25 to 0.25
- value_weight: bfloat16 [576, 192], replicated, may hold values from -0.25 to 0.25
- out_weight: bfloat16 [576, 576], replicated, may hold values from -2 to 2
- gain_mlp: bfloat16 [576], replicated, may hold values from 0.5 to 1.5
- gate_weight: bfloat16 [576, 1536], replicated, may hold values from -0.25 to 0.25
- up_weight: bfloat16 [576, 1536], replicated, may hold values from -0.25 to 0.25
- down_weight: bfloat16 [1536, 576], replicated, may hold values from -0.15625 to 0.15625
- cotangent: bfloat16 [32, 2, 512, 576], P('batch', None, 'seq'), may hold values from -6 to 6
Outputs:
- block_out: bfloat16 [32, 2, 512, 576], P('batch', None, 'seq')
- input_grad: float32 [32, 2, 512, 576], P('batch', None, 'seq')
- grad_gain_attn: float32 [576], replicated
- grad_query: float32 [576, 576], replicated
- grad_key: float32 [576, 192], replicated
- grad_value: float32 [576, 192], replicated
- grad_out: float32 [576, 576], replicated
- grad_gain_mlp: float32 [576], replicated
- grad_gate: float32 [576, 1536], replicated
- grad_up: float32 [576, 1536], replicated
- grad_down: float32 [1536, 576], replicated
Inputs may be any that keep to these rules, and one draw needn't show every extreme that they name: A permutation; batch slot s holds sequence assign[s]. `lengths`: in each block of 8 consecutive batch slots some slot holds a sequence of length 1024; some sequence has length 128.
All inputs are finite; a program needn't handle non-finite values.
Results may differ from a plain program's by a relative error of at most 0.015.
Values may be sent and summed in bfloat16 or wider, within the bound.
No kernel may reach another device: no remote copies, remote signals or barrier semaphores. Data moves between devices by JAX's collectives and lax.ppermute only.
A program may use at most 256 MiB of HBM per device.

v0:
```python
import jax
import jax.numpy as jnp
from jax import lax
from jax.sharding import PartitionSpec as P

HEADS = 9
KV_HEADS = 3
HEAD_DIM = 64


epsilon = 1e-06
rope_base = 10000.0
masked_score = -1e30


def matmul(left, right):
    return jnp.dot(left, right, preferred_element_type=jnp.float32)


def weight_grad(left, right):
    return lax.dot_general(
        left, right, (((0,), (0,)), ((), ())), preferred_element_type=jnp.float32
    )


def through(left, right):
    return lax.dot_general(
        left, right, (((1,), (1,)), ((), ())), preferred_element_type=jnp.float32
    )


def rotate(tensor, cosine, sine):
    half_dim = tensor.shape[-1] // 2
    first_half = tensor[..., :half_dim]
    second_half = tensor[..., half_dim:]
    return jnp.concatenate(
        [first_half * cosine - second_half * sine, second_half * cosine + first_half * sine],
        axis=-1,
    )


def rotate_back(incoming, cosine, sine):
    half_dim = incoming.shape[-1] // 2
    first_half = incoming[..., :half_dim]
    second_half = incoming[..., half_dim:]
    return jnp.concatenate(
        [first_half * cosine + second_half * sine, second_half * cosine - first_half * sine],
        axis=-1,
    )


def angles_of(positions):
    frequency = jnp.power(rope_base, -2.0 * jnp.arange(HEAD_DIM // 2, dtype=jnp.float32) / HEAD_DIM)
    angles = positions.astype(jnp.float32)[..., None] * frequency
    return (jnp.cos(angles)[:, :, None, :], jnp.sin(angles)[:, :, None, :])


def norm_forward(values, gain):
    inverse = lax.rsqrt(jnp.mean(values * values, axis=-1, keepdims=True) + epsilon)
    return (inverse, (values * inverse * gain).astype(jnp.bfloat16))


def norm_backward(incoming, values, inverse, gain):
    scaled = incoming * gain
    gain_part = jnp.sum(incoming * values * inverse, axis=(0, 1, 2))
    value_part = inverse * scaled - values * inverse**3 * jnp.mean(
        scaled * values, axis=-1, keepdims=True
    )
    return (value_part, gain_part)


def scores_for(query_s, packed_s, length_s, query_pos, key_pos):
    group_size = HEADS // KV_HEADS
    key_width = KV_HEADS * HEAD_DIM
    query_rows = query_s.reshape(-1, KV_HEADS, group_size, HEAD_DIM)
    key_rows = packed_s[..., :key_width].reshape(-1, KV_HEADS, HEAD_DIM)
    value_rows = packed_s[..., key_width:].reshape(-1, KV_HEADS, HEAD_DIM)
    raw_scores = jnp.einsum(
        "qcgd,kcd->cgqk", query_rows, key_rows, preferred_element_type=jnp.float32
    )
    query_place = query_pos.reshape(-1)
    key_place = key_pos.reshape(-1)
    allowed = (key_place[None, :] <= query_place[:, None]) & (key_place[None, :] < length_s)
    scores = jnp.where(allowed, raw_scores * HEAD_DIM ** (-0.5), masked_score)
    return (scores, query_rows, key_rows, value_rows)


def attend_one(inputs, local_pos, key_pos):
    query_s, packed_s, length_s = inputs
    scores, query_rows, key_rows, value_rows = scores_for(
        query_s, packed_s, length_s, local_pos, key_pos
    )
    row_top = jnp.max(scores, axis=-1, keepdims=True)
    shifted = jnp.exp(scores - row_top)
    row_total = jnp.sum(shifted, axis=-1, keepdims=True)
    soft_probs = (shifted / row_total).astype(jnp.bfloat16)
    result = jnp.einsum(
        "cgqk,kcd->qcgd", soft_probs, value_rows, preferred_element_type=jnp.float32
    )
    return (result.reshape(query_s.shape[:2] + (-1,)), row_top + jnp.log(row_total))


def attend_back(inputs, query_pos, key_pos):
    query_s, packed_s, length_s, log_total, grad_attn = inputs[:5]
    scores, query_rows, key_rows, value_rows = scores_for(
        query_s, packed_s, length_s, query_pos, key_pos
    )
    soft_probs = jnp.exp(scores - log_total)
    grad_rows = grad_attn.reshape(query_rows.shape)
    grad_probs = jnp.einsum(
        "qcgd,kcd->cgqk", grad_rows, value_rows, preferred_element_type=jnp.float32
    )
    inner = jnp.sum(soft_probs * grad_probs, axis=-1, keepdims=True)
    grad_raw = (soft_probs * (grad_probs - inner) * HEAD_DIM ** (-0.5)).astype(jnp.bfloat16)
    results = ()
    grad_query = jnp.einsum(
        "cgqk,kcd->qcgd", grad_raw, key_rows, preferred_element_type=jnp.float32
    )
    results = results + (grad_query.reshape(query_s.shape),)
    grad_keys = jnp.einsum(
        "cgqk,qcgd->kcd", grad_raw, query_rows, preferred_element_type=jnp.float32
    )
    grad_values = jnp.einsum(
        "cgqk,qcgd->kcd",
        soft_probs.astype(jnp.bfloat16),
        grad_rows,
        preferred_element_type=jnp.float32,
    )
    key_count = key_rows.shape[0]
    grad_packed = jnp.concatenate(
        [grad_keys.reshape(key_count, -1), grad_values.reshape(key_count, -1)], axis=-1
    )
    results = results + (grad_packed.reshape(packed_s.shape),)
    return results


def front_half(residual, attn_gain, query_weight, key_weight, value_weight, cosine, sine):
    inverse, normed = norm_forward(residual, attn_gain)
    lead_shape = residual.shape[:3]
    flat_rows = normed.reshape(-1, residual.shape[-1])
    query_heads = rotate(
        matmul(flat_rows, query_weight).reshape(lead_shape + (HEADS, HEAD_DIM)), cosine, sine
    ).astype(jnp.bfloat16)
    key_heads = rotate(
        matmul(flat_rows, key_weight).reshape(lead_shape + (KV_HEADS, HEAD_DIM)), cosine, sine
    ).astype(jnp.bfloat16)
    value_rows = matmul(flat_rows, value_weight).astype(jnp.bfloat16)
    packed = jnp.concatenate(
        [key_heads.reshape(lead_shape + (-1,)), value_rows.reshape(lead_shape + (-1,))], axis=-1
    )
    return (inverse, flat_rows, query_heads, packed)


def rear_half(
    residual,
    query_heads,
    gathered,
    seq_lens,
    local_pos,
    key_pos,
    mlp_gain,
    out_weight,
    gate_weight,
    up_weight,
    down_weight,
):
    features = residual.shape[-1]
    attended, log_total = lax.map(
        lambda inputs: attend_one(inputs, local_pos, key_pos), (query_heads, gathered, seq_lens)
    )
    attn_rows = attended.astype(jnp.bfloat16).reshape(-1, features)
    middle = residual + matmul(attn_rows, out_weight).reshape(residual.shape)
    mlp_inverse, mlp_normed = norm_forward(middle, mlp_gain)
    mlp_rows = mlp_normed.reshape(-1, features)
    gate_proj = matmul(mlp_rows, gate_weight)
    up_proj = matmul(mlp_rows, up_weight)
    activated = (jax.nn.silu(gate_proj) * up_proj).astype(jnp.bfloat16)
    mlp_out = matmul(activated, down_weight).reshape(residual.shape)
    return (
        log_total,
        attn_rows,
        middle,
        mlp_inverse,
        mlp_rows,
        gate_proj,
        up_proj,
        activated,
        mlp_out,
    )


def shards(
    tokens,
    assign,
    lengths,
    gain_attn,
    query_weight,
    key_weight,
    value_weight,
    out_weight,
    gain_mlp,
    gate_weight,
    up_weight,
    down_weight,
    cotangent,
):
    span_len = tokens.shape[2]
    features = tokens.shape[3]
    key_width = KV_HEADS * HEAD_DIM
    half_len = span_len * lax.axis_size("seq")
    full_len = 2 * half_len
    my_index = lax.axis_index("seq")
    row_index = my_index * span_len + jnp.arange(span_len, dtype=jnp.int32)
    local_pos = jnp.stack([row_index, full_len - 1 - row_index])
    all_index = jnp.arange(half_len, dtype=jnp.int32)
    key_pos = jnp.stack([all_index, full_len - 1 - all_index])
    matches = assign[:, None] == jnp.arange(lengths.shape[0], dtype=jnp.int32)[None, :]
    seq_lens = jnp.sum(jnp.where(matches, lengths[None, :], 0), axis=1)
    valid = (local_pos[None, :, :] < seq_lens[:, None, None])[..., None]
    cosine, sine = angles_of(local_pos)
    attn_gain = gain_attn.astype(jnp.float32)
    mlp_gain = gain_mlp.astype(jnp.float32)
    residual = tokens.astype(jnp.float32)
    inverse, flat_rows, query_heads, packed = front_half(
        residual, attn_gain, query_weight, key_weight, value_weight, cosine, sine
    )
    gathered = lax.all_gather(packed, "seq", axis=2, tiled=True)
    log_total, attn_rows, middle, mlp_inverse, mlp_rows, gate_proj, up_proj, activated, mlp_out = (
        rear_half(
            residual,
            query_heads,
            gathered,
            seq_lens,
            local_pos,
            key_pos,
            mlp_gain,
            out_weight,
            gate_weight,
            up_weight,
            down_weight,
        )
    )
    block_out = jnp.where(valid, middle + mlp_out, 0.0).astype(jnp.bfloat16)
    incoming = jnp.where(valid, cotangent, jnp.zeros_like(cotangent))
    tokens_again, incoming = lax.optimization_barrier((tokens, incoming))
    residual = tokens_again.astype(jnp.float32)
    inverse, flat_rows, query_heads, packed = front_half(
        residual, attn_gain, query_weight, key_weight, value_weight, cosine, sine
    )
    gathered = lax.all_gather(packed, "seq", axis=2, tiled=True)
    log_total, attn_rows, middle, mlp_inverse, mlp_rows, gate_proj, up_proj, activated, mlp_out = (
        rear_half(
            residual,
            query_heads,
            gathered,
            seq_lens,
            local_pos,
            key_pos,
            mlp_gain,
            out_weight,
            gate_weight,
            up_weight,
            down_weight,
        )
    )
    incoming_rows = incoming.reshape(-1, features)
    grad_down = weight_grad(activated, incoming_rows)
    grad_act = through(incoming_rows, down_weight)
    sigmoid_gate = jax.nn.sigmoid(gate_proj)
    back_gate = (
        grad_act * up_proj * sigmoid_gate * (1.0 + gate_proj * (1.0 - sigmoid_gate))
    ).astype(jnp.bfloat16)
    back_up = (grad_act * gate_proj * sigmoid_gate).astype(jnp.bfloat16)
    grad_gate = weight_grad(mlp_rows, back_gate)
    grad_up = weight_grad(mlp_rows, back_up)
    back_normed_mlp = through(back_gate, gate_weight) + through(back_up, up_weight)
    back_middle, grad_gain_mlp = norm_backward(
        back_normed_mlp.reshape(middle.shape), middle, mlp_inverse, mlp_gain
    )
    back_middle = back_middle + incoming.astype(jnp.float32)
    back_attn = back_middle.astype(jnp.bfloat16).reshape(-1, features)
    grad_out = weight_grad(attn_rows, back_attn)
    back_attended = through(back_attn, out_weight).astype(jnp.bfloat16).reshape(tokens.shape)
    back_query, back_packed_all = lax.map(
        lambda inputs: attend_back(inputs, local_pos, key_pos),
        (query_heads, gathered, seq_lens, log_total, back_attended),
    )
    back_packed = lax.psum_scatter(
        back_packed_all.astype(jnp.bfloat16), "seq", scatter_dimension=2, tiled=True
    ).astype(jnp.float32)
    lead_shape = tokens.shape[:3]
    back_keys = rotate_back(
        back_packed[..., :key_width].reshape(lead_shape + (KV_HEADS, HEAD_DIM)), cosine, sine
    )
    back_keys = back_keys.astype(jnp.bfloat16).reshape(-1, key_width)
    back_values = back_packed[..., key_width:].astype(jnp.bfloat16).reshape(-1, key_width)
    back_queries = rotate_back(back_query, cosine, sine).astype(jnp.bfloat16).reshape(-1, features)
    grad_query = weight_grad(flat_rows, back_queries)
    grad_key = weight_grad(flat_rows, back_keys)
    grad_value = weight_grad(flat_rows, back_values)
    back_normed = (
        through(back_queries, query_weight)
        + through(back_keys, key_weight)
        + through(back_values, value_weight)
    )
    back_input, grad_gain_attn = norm_backward(
        back_normed.reshape(residual.shape), residual, inverse, attn_gain
    )
    input_grad = back_input + back_middle
    (
        grad_gain_attn,
        grad_query,
        grad_key,
        grad_value,
        grad_out,
        grad_gain_mlp,
        grad_gate,
        grad_up,
        grad_down,
    ) = lax.psum(
        (
            grad_gain_attn,
            grad_query,
            grad_key,
            grad_value,
            grad_out,
            grad_gain_mlp,
            grad_gate,
            grad_up,
            grad_down,
        ),
        ("seq", "batch"),
    )
    return (
        block_out,
        input_grad,
        grad_gain_attn,
        grad_query,
        grad_key,
        grad_value,
        grad_out,
        grad_gain_mlp,
        grad_gate,
        grad_up,
        grad_down,
    )


def solution(mesh):
    return jax.shard_map(
        shards,
        mesh=mesh,
        in_specs=(
            P("batch", None, "seq", None),
            P("batch"),
            P(),
            P(),
            P(),
            P(),
            P(),
            P(),
            P(),
            P(),
            P(),
            P(),
            P("batch", None, "seq", None),
        ),
        out_specs=(
            P("batch", None, "seq", None),
            P("batch", None, "seq", None),
            P(),
            P(),
            P(),
            P(),
            P(),
            P(),
            P(),
            P(),
            P(),
        ),
        check_vma=False,
    )
```

profile of v0, /device:TPU:0, one launch (start us, length us, event | category | flops | bytes accessed | tf_op | source)
XLA Modules:
  0.0 1049.2 jit_solution(6592610671387124028)
XLA Ops:
  34.0 3.7 fusion.81
  43.2 3.8 copy.105
  47.1 52.0 %all-gather.5.cloned.1.call-done = bf16[8,2,512,384]{3,2,1,0:T(8,128)(2,1)} async-done(((bf16[8,2,64,384]{3,2,1,0:T(8,128)(2,1)}), bf16[8,2,512,384]{3,2,1,0:T(8,128)(2,1)}) %all-gather.5.cloned.1.call-update) | async-done | bytes 6291472 | tf_op jit(solution)/shard_map/all_gather | solution.py:250
  99.0 16.1 %copy.104 = bf16[8,2,512,384]{2,1,3,0:T(2,128)(2,1)} copy(bf16[8,2,512,384]{3,2,1,0:T(8,128)(2,1)} %all-gather.5.cloned.1.call-done) | data formatting | bytes 12582912 | tf_op jit(solution)/shard_map/while | solution.py:284
  117.8 132.7 %while.38 = (s32[]{:T(128)}, bf16[8,2,64,576]{2,1,3,0:T(2,128)(2,1)}, f32[8,3,3,128,1]{3,2,1,4,0:T(4,128)}, bf16[8,2,512,384]{2,1,3,0:T(2,128)(2,1)}, s32[2,512]...) while((s32[]{:T(128)}, ...), condition=%wide.wide.region_11.12_spmd, body=%wide.wide.region_8.11_spmd.sunk | while | flops 316407680 | bytes 23961796 | solution.py:168
  250.5 6.3 copy.101
  266.9 4.4 multiply_convert_fusion.1
  274.0 3.4 convolution_add_fusion
  277.4 3.2 copy.102
  280.6 4.7 multiply_reduce_fusion
  290.0 339.5 %while.39 = (s32[]{:T(128)}, f32[8,2,64,9,64]{2,4,3,1,0:T(8,128)}, bf16[8,2,512,384]{3,2,1,0:T(8,128)(2,1)}, bf16[8,2,512,384]{2,1,3,0:T(2,128)(2,1)}, s32[2,512...) while((s32[]{:T(128)}, f32[8,2,64,9,64]{2,4,3,1,0:T(8,128)}, ...), condition=%wide.wide.region_16.17_spmd, body=%wide.wide.region_14.16_spmd.sunk | while | flops 786306304 | bytes 50406564 | solution.py:284
  304.0 10.1 convolution_bitcast_fusion.8
  314.1 9.5 convolution_bitcast_fusion.9
  323.6 3.6 fusion.232
  346.3 10.1 convolution_bitcast_fusion.8
  356.5 9.5 convolution_bitcast_fusion.9
  365.9 3.6 fusion.232
  388.7 10.1 convolution_bitcast_fusion.8
  398.8 9.5 convolution_bitcast_fusion.9
  408.3 3.6 fusion.232
  431.0 10.2 convolution_bitcast_fusion.8
  441.2 9.5 convolution_bitcast_fusion.9
  450.7 3.6 fusion.232
  473.4 10.2 convolution_bitcast_fusion.8
  483.5 9.5 convolution_bitcast_fusion.9
  493.0 3.6 fusion.232
  515.7 10.1 convolution_bitcast_fusion.8
  525.9 9.5 convolution_bitcast_fusion.9
  535.3 3.6 fusion.232
  558.1 10.1 convolution_bitcast_fusion.8
  568.2 9.5 convolution_bitcast_fusion.9
  577.7 3.6 fusion.232
  600.6 10.1 convolution_bitcast_fusion.8
  610.7 9.5 convolution_bitcast_fusion.9
  620.2 3.6 fusion.232
  640.7 3.5 pad_maximum_fusion.1
  645.6 3.8 copy.109
  649.4 6.5 convert_element_type.147
  656.0 3.8 fusion.106
  662.6 3.9 fusion.108
  666.5 3.9 fusion.107
  671.0 4.2 fusion.59
  675.2 23.1 %reduce-scatter.2.cloned.1.call-done = bf16[8,2,64,384]{3,2,1,0:T(8,128)(2,1)} async-done(((bf16[8,2,512,384]{3,2,1,0:T(8,128)(2,1)}), bf16[8,2,64,384]{3,2,1,0:T(8,128)(2,1)}) %reduce-scatter.2.cloned.1.call-update) | async-done | bytes 786448 | tf_op jit(solution)/shard_map/reduce_scatter | solution.py:288
  707.5 3.1 convert_element_type.150
  714.6 48.4 %all-gather.3.cloned.1.call-done = bf16[8,2,512,384]{3,2,1,0:T(8,128)(2,1)} async-done(((bf16[8,2,64,384]{3,2,1,0:T(8,128)(2,1)}), bf16[8,2,512,384]{3,2,1,0:T(8,128)(2,1)}) %all-gather.3.cloned.1.call-update) | async-done | bytes 6291472 | tf_op jit(solution)/shard_map/all_gather | solution.py:227
  765.6 124.0 %while.37 = (s32[]{:T(128)}, bf16[8,2,64,576]{2,1,3,0:T(2,128)(2,1)}, bf16[8,2,512,384]{3,2,1,0:T(8,128)(2,1)}, s32[2,512]{1,0:T(2,128)S(1)}, s32[2,64]{1,0:T(2,...) while((s32[]{:T(128)}, ...), condition=%wide.wide.region_5.6_spmd, body=%wide.wide.region_2.5_spmd.sunk | while | flops 309331968 | bytes 18722432 | solution.py:168
  772.3 4.7 fusion.213
  787.8 4.7 fusion.213
  803.3 4.7 fusion.213
  818.8 4.7 fusion.213
  834.4 4.7 fusion.213
  839.1 3.0 fusion.214
  850.0 4.7 fusion.213
  865.4 4.7 fusion.213
  880.9 4.7 fusion.213
  889.6 5.5 multiply_reduce_fusion.3
  899.3 3.5 copy.113
  902.9 3.6 fusion.71
  906.5 41.1 %all-reduce = (f32[576]{0:T(1024)}, f32[576]{0:T(1024)}) all-reduce(f32[576]{0:T(1024)S(1)} %get-tuple-element.230, f32[576]{0:T(1024)S(1)} %copy-done.60), channel_id=1, replica_groups=mesh['seq'=8,'batch'=4] {'seq','batch'}, use_global_device_ids=true, to_apply=%region_20.21 | all-reduce | flops 1152 | bytes 9216 | tf_op jit(solution)/shard_map/psum | solution.py:320
  947.7 7.7 fusion.68
  956.4 4.6 fusion.100
  961.0 10.5 %fusion.74 = f32[1024,576]{1,0:T(8,128)} fusion(bf16[1536,576]{0,1:T(8,128)(2,1)} %param.30, f32[1024,1536]{1,0:T(8,128)} %fusion.100, bf16[1024,576]{1,0:T(8,128)(2,1)} %bitcast.450, bf16[576,1536]{1,0:T(8,128)(2,1)S(1)} %copy-done.65), kind=kOutput, calls=%fused_computation.125 | convolution fusion | flops 3633315840 | bytes 13369344 | tf_op jit(solution)/shard_map/dot_general | solution.py:17
  971.5 3.9 select_convert_fusion
  975.5 53.3 %all-reduce.4.cloned.1.call-done = (f32[576,576]{1,0:T(8,128)}, f32[576,192]{0,1:T(8,128)}, f32[576,192]{0,1:T(8,128)}, f32[576,576]{1,0:T(8,128)}, f32[576,1536...) async-done(((f32[576,576]{1,0:T(8,128)}, f32[576,192]{0,1:T(8,128)}, f32[576,192]{0,1:T(8,128)}, f32[576,576]{1,0:T(8,128)}, f32[576,1536]{1,0:T(8,128)}, ...) | async-done | bytes 14155792 | tf_op jit(solution)/shard_map/psum | solution.py:320
  (697 shorter events, 470.2 us)
Async XLA Ops:
  7.2 252.9 %copy-start = (bf16[576,1536]{1,0:T(8,128)(2,1)S(1)}, bf16[576,1536]{1,0:T(8,128)(2,1)}, u32[]{:S(2)}) copy-start(bf16[576,1536]{1,0:T(8,128)(2,1)} %param.28) | copy-start | bytes 5308420
  7.2 6.3 copy-start.2
  7.2 91.8 %all-gather.5.cloned.1.call-start = ((), (), s32[]{:S(2)}) async-start(), calls=%async_computation.2 | async-start | bytes 7077888 | tf_op jit(solution)/shard_map/all_gather | solution.py:250
  8.2 6.3 copy-start.55
  10.7 20.9 %copy-start.61 = (s32[2,64]{1,0:T(2,128)}, s32[2,64]{1,0:T(2,128)S(1)}, u32[]{:S(2)}) copy-start(s32[2,64]{1,0:T(2,128)S(1)} %get-tuple-element.702) | copy-start | bytes 1540
  10.8 3.7 copy-start.57
  13.5 4.3 copy-start.26
  15.1 6.1 copy-start.24
  24.3 15.3 %copy-start.37 = (f32[2,64,32]{1,2,0:T(8,128)}, f32[2,64,32]{1,2,0:T(8,128)S(1)}, u32[]{:S(2)}) copy-start(f32[2,64,32]{1,2,0:T(8,128)S(1)} %get-tuple-element.329) | copy-start | bytes 49156
  24.4 15.3 %copy-start.39 = (f32[2,64,32]{1,2,0:T(8,128)}, f32[2,64,32]{1,2,0:T(8,128)S(1)}, u32[]{:S(2)}) copy-start(f32[2,64,32]{1,2,0:T(8,128)S(1)} %get-tuple-element.330) | copy-start | bytes 49156
  25.7 6.0 copy-start.63
  31.5 666.8 %reduce-scatter.2.cloned.1.call-start = ((), (), s32[]{:S(2)}) async-start(), calls=%async_computation.3 | async-start | bytes 7077888 | tf_op jit(solution)/shard_map/reduce_scatter | solution.py:288
  31.7 253.7 %copy-start.49 = (f32[576]{0:T(1024)}, f32[576]{0:T(1024)S(1)}, u32[]{:S(2)}) copy-start(f32[576]{0:T(1024)S(1)} %convert_element_type.131) | copy-start | bytes 6916
  34.0 3.7 copy-start.7
  34.0 3.7 copy-start.42
  259.7 3.0 copy-start.4
  259.7 25.6 %copy-start.45 = (f32[8,2,64]{2,1,0:T(2,128)}, f32[8,2,64]{2,1,0:T(2,128)S(1)}, u32[]{:S(2)}) copy-start(f32[8,2,64]{2,1,0:T(2,128)S(1)} %get-tuple-element.324) | copy-start | bytes 12292
  259.7 25.6 %copy-start.51 = (f32[8,2,64]{2,1,0:T(2,128)}, f32[8,2,64]{2,1,0:T(2,128)S(1)}, u32[]{:S(2)}) copy-start(f32[8,2,64]{2,1,0:T(2,128)S(1)} %get-tuple-element.323) | copy-start | bytes 12292
  260.1 2.6 copy-start.33
  260.1 2.6 copy-start.64
  262.7 3.2 copy-start.71
  262.7 3.2 copy-start.10
  262.7 4.2 copy-start.66
  265.4 5.9 copy-start.72
  271.3 2.7 copy-start.69
  280.6 4.8 copy-start.1
  280.6 4.8 copy-start.5
  629.6 133.4 %all-gather.3.cloned.1.call-start = ((), (), s32[]{:S(2)}) async-start(), calls=%async_computation.1 | async-start | bytes 7077888 | tf_op jit(solution)/shard_map/all_gather | solution.py:227
  633.4 7.2 copy-start.62
  633.4 7.3 copy-start.16
  640.5 3.7 copy-start.38
  640.5 3.7 copy-start.40
  640.6 388.2 %all-reduce.4.cloned.1.call-start = ((), (), s32[]{:S(2)}) async-start(), calls=%async_computation.4 | async-start | bytes 29097984 | tf_op jit(solution)/shard_map/psum | solution.py:320
  640.7 3.6 copy-start.17
  649.4 6.6 copy-start.8
  656.0 3.8 copy-start.32
  656.0 3.8 copy-start.36
  659.7 2.9 copy-start.70
  662.6 3.9 copy-start.68
  662.6 7.7 slice-start
  662.6 7.7 slice-start.2
  666.5 3.9 copy-start.11
  666.5 3.9 slice-start.1
  666.5 4.5 slice-start.3
  710.6 4.0 copy-start.21
  889.5 5.5 copy-start.22
  889.6 5.5 copy-start.25
  899.3 3.5 copy-start.3
  899.3 3.5 copy-start.48
  899.3 3.5 copy-start.56
  902.8 3.7 copy-start.60
  902.8 44.8 %copy-start.46 = (f32[8,2,64]{2,1,0:T(2,128)S(1)}, f32[8,2,64]{2,1,0:T(2,128)}, u32[]{:S(2)}) copy-start(f32[8,2,64]{2,1,0:T(2,128)} %copy-done.45) | copy-start | bytes 12292
  902.8 44.8 %copy-start.50 = (f32[576]{0:T(1024)S(1)}, f32[576]{0:T(1024)}, u32[]{:S(2)}) copy-start(f32[576]{0:T(1024)} %copy-done.49) | copy-start | bytes 6916
  902.9 44.8 %copy-start.52 = (f32[8,2,64]{2,1,0:T(2,128)S(1)}, f32[8,2,64]{2,1,0:T(2,128)}, u32[]{:S(2)}) copy-start(f32[8,2,64]{2,1,0:T(2,128)} %copy-done.51) | copy-start | bytes 12292
  902.9 44.8 %copy-start.54 = (f32[8,2,64]{2,1,0:T(2,128)S(1)}, f32[8,2,64]{2,1,0:T(2,128)}, u32[]{:S(2)}) copy-start(f32[8,2,64]{2,1,0:T(2,128)} %copy-done.53) | copy-start | bytes 12292
  902.9 44.8 %copy-start.59 = (f32[8,2,64]{2,1,0:T(2,128)S(1)}, f32[8,2,64]{2,1,0:T(2,128)}, u32[]{:S(2)}) copy-start(f32[8,2,64]{2,1,0:T(2,128)} %get-tuple-element.321) | copy-start | bytes 12292
  956.4 4.6 copy-start.65
  961.0 10.5 %copy-start.58 = (pred[8,2,64]{2,1,0:T(4,128)(4,1)S(1)}, pred[8,2,64]{2,1,0:T(4,128)(4,1)}, u32[]{:S(2)}) copy-start(pred[8,2,64]{2,1,0:T(4,128)(4,1)} %copy-done.57) | copy-start | bytes 3076
  1028.8 2.7 copy-start.44
  1028.8 3.5 copy-start.43
  1028.8 4.3 copy-start.30
  1031.5 2.7 copy-start.20
  1034.2 3.3 copy-start.19
  1037.5 3.3 copy-start.18
  (31 other events, 44.8 us)
Sparse Core Ops, SparseCore 0:
  31.6 67.4 all-gather.4
  629.7 68.5 reduce-scatter.1
  699.9 63.0 all-gather.2
  770.4 258.3 all-reduce.3
where the time goes:
time: 1060 us; the launch traced here: 1050 us
  matrix products  397 us (37%)
  local copies, waits for them, and re-layouts  310 us (29%)
  waiting for transfers between devices  177 us (17%)
  other arithmetic  108 us (10%)
  blocking collectives  41.1 us (4%)
  between operations  14.7 us (1%)
    all_gather x2, waiting for transfers between devices, shards(): gathered = lax.all_gather(packed, 'seq', axis=2, tiled=True)  100 us
    dot_general x8, matrix products, attend_back(): jnp.einsum('cgqk,kcd->qcgd', grad_raw, key_rows, preferred_element_type=j...  81.2 us
    dot_general x8, matrix products, attend_back(): jnp.einsum('cgqk,qcgd->kcd', grad_raw, query_rows, preferred_element_type...  75.8 us
    dynamic_slice x72, local copies, waits for them, and re-layouts, rear_half(): lax.map(lambda inputs: attend_one(inputs, local_pos, key_pos), (query_hea...  59.2 us
    psum x1, waiting for transfers between devices, shards(): lax.psum((grad_gain_attn, grad_query, grad_key, grad_value, grad_out, gra...  53.3 us
    psum x1, blocking collectives, shards(): lax.psum((grad_gain_attn, grad_query, grad_key, grad_value, grad_out, gra...  41.1 us
    dot_general x12, matrix products, matmul(): return jnp.dot(left, right, preferred_element_type=jnp.float32)  40 us
    dot_general x16, matrix products, scores_for(): jnp.einsum('qcgd,kcd->cgqk', query_rows, key_rows, preferred_element_type...  38.8 us
  transfers between devices with their start and end apart: 4, of which 4 were waited for; matrix products, arithmetic and copies ran while one was open for 23% of the time, Pallas kernels for 0%

commit v1 on v0

--- a/solution.py
+++ b/solution.py
@@ -242,27 +242,6 @@
     )
     block_out = jnp.where(valid, middle + mlp_out, 0.0).astype(jnp.bfloat16)
     incoming = jnp.where(valid, cotangent, jnp.zeros_like(cotangent))
-    tokens_again, incoming = lax.optimization_barrier((tokens, incoming))
-    residual = tokens_again.astype(jnp.float32)
-    inverse, flat_rows, query_heads, packed = front_half(
-        residual, attn_gain, query_weight, key_weight, value_weight, cosine, sine
-    )
-    gathered = lax.all_gather(packed, "seq", axis=2, tiled=True)
-    log_total, attn_rows, middle, mlp_inverse, mlp_rows, gate_proj, up_proj, activated, mlp_out = (
-        rear_half(
-            residual,
-            query_heads,
-            gathered,
-            seq_lens,
-            local_pos,
-            key_pos,
-            mlp_gain,
-            out_weight,
-            gate_weight,
-            up_weight,
-            down_weight,
-        )
-    )
     incoming_rows = incoming.reshape(-1, features)
     grad_down = weight_grad(activated, incoming_rows)
     grad_act = through(incoming_rows, down_weight)
@@ -307,30 +286,12 @@
         back_normed.reshape(residual.shape), residual, inverse, attn_gain
     )
     input_grad = back_input + back_middle
-    (
-        grad_gain_attn,
-        grad_query,
-        grad_key,
-        grad_value,
-        grad_out,
-        grad_gain_mlp,
-        grad_gate,
-        grad_up,
-        grad_down,
-    ) = lax.psum(
-        (
-            grad_gain_attn,
-            grad_query,
-            grad_key,
-            grad_value,
-            grad_out,
-            grad_gain_mlp,
-            grad_gate,
-            grad_up,
-            grad_down,
-        ),
-        ("seq", "batch"),
-    )
+    names = (grad_query, grad_key, grad_value, grad_out, grad_gate, grad_up, grad_down)
+    sums = lax.psum(tuple(g.astype(jnp.bfloat16) for g in names), ("seq", "batch"))
+    grad_query, grad_key, grad_value, grad_out, grad_gate, grad_up, grad_down = (
+        g.astype(jnp.float32) for g in sums
+    )
+    grad_gain_attn, grad_gain_mlp = lax.psum((grad_gain_attn, grad_gain_mlp), ("seq", "batch"))
     return (
         block_out,
         input_grad,

time: 1060 us -> 850 us (0.80)
  local copies, waits for them, and re-layouts: 310 us -> 195 us
  matrix products: 397 us -> 308 us
  other arithmetic: 108 us -> 81.6 us
  waiting for transfers between devices: 177 us -> 199 us
    psum x1, waiting for transfers between devices: 53.3 us -> 106 us  [shards(): lax.psum(tuple((g.astype(jnp.bfloat16) for g in names)), ('seq', 'batch'))]
    all_gather x2 -> x1, waiting for transfers between devices: 100 us -> 55 us  [shards(): gathered = lax.all_gather(packed, 'seq', axis=2, tiled=True)]
    sub x8 -> x0, matrix products: 37.7 us -> none  [attend_one(): shifted = jnp.exp(scores - row_top)]
    dynamic_slice x72 -> x32, local copies, waits for them, and re-layouts: 59.2 us -> 28.3 us  [rear_half(): lax.map(lambda inputs: attend_one(inputs, local_pos, key_pos), (query_hea...]
    dot_general x16 -> x8, matrix products: 34.4 us -> 11.2 us  [attend_one(): jnp.einsum('cgqk,kcd->qcgd', soft_probs, value_rows, preferred_element_ty...]
    dot_general x12 -> x7, matrix products: 40 us -> 19.6 us  [matmul(): return jnp.dot(left, right, preferred_element_type=jnp.float32)]
    reshape x24 -> x16, local copies, waits for them, and re-layouts: 20.3 us -> 4.3 us  [scores_for(): value_rows = packed_s[..., key_width:].reshape(-1, KV_HEADS, HEAD_DIM)]
    unnamed x158 -> x97, local copies, waits for them, and re-layouts: 25.4 us -> 9.52 us
  transfers between devices with their start and end apart: 4 -> 3, of which waited for: 4 -> 3; matrix products, arithmetic and copies ran while one was open for 23% -> 8% of each run, Pallas kernels for 0% -> 0%
where the time goes in v1:
time: 850 us; the launch traced here: 840 us
  matrix products  308 us (36%)
  waiting for transfers between devices  199 us (23%)
  local copies, waits for them, and re-layouts  195 us (23%)
  other arithmetic  81.6 us (10%)
  blocking collectives  39.3 us (5%)
  between operations  14.5 us (2%)
    psum x1, waiting for transfers between devices, shards(): lax.psum(tuple((g.astype(jnp.bfloat16) for g in names)), ('seq', 'batch'))  106 us
    dot_general x8, matrix products, attend_back(): jnp.einsum('cgqk,kcd->qcgd', grad_raw, key_rows, preferred_element_type=j...  81.5 us
    dot_general x8, matrix products, attend_back(): jnp.einsum('cgqk,qcgd->kcd', grad_raw, query_rows, preferred_element_type...  76.1 us
    all_gather x1, waiting for transfers between devices, shards(): gathered = lax.all_gather(packed, 'seq', axis=2, tiled=True)  55 us
    psum x1, blocking collectives, shards(): lax.psum((grad_gain_attn, grad_gain_mlp), ('seq', 'batch'))  39.3 us
    reduce_scatter x1, waiting for transfers between devices, shards(): lax.psum_scatter(back_packed_all.astype(jnp.bfloat16), 'seq', scatter_dim...  37.7 us
    dot_general x16, matrix products, scores_for(): jnp.einsum('qcgd,kcd->cgqk', query_rows, key_rows, preferred_element_type...  31 us
    dot_general x8, matrix products, attend_back(): jnp.einsum('cgqk,qcgd->kcd', soft_probs.astype(jnp.bfloat16), grad_rows,...  28.8 us
  transfers between devices with their start and end apart: 3, of which 3 were waited for; matrix products, arithmetic and copies ran while one was open for 8% of the time, Pallas kernels for 0%

profile of v1, /device:TPU:0, one launch (start us, length us, event | category | flops | bytes accessed | tf_op | source)
XLA Modules:
  0.0 839.8 jit_solution(15835649801397779462)
XLA Ops:
  24.3 3.1 fusion.49
  28.8 3.9 copy.78
  34.3 55.0 %all-gather.2.cloned.1.call-done = bf16[8,2,512,384]{3,2,1,0:T(8,128)(2,1)} async-done(((bf16[8,2,64,384]{3,2,1,0:T(8,128)(2,1)}), bf16[8,2,512,384]{3,2,1,0:T(8,128)(2,1)}) %all-gather.2.cloned.1.call-update) | async-done | bytes 6291472 | tf_op jit(solution)/shard_map/all_gather | solution.py:227
  89.3 16.5 %copy.77 = bf16[8,2,512,384]{2,1,3,0:T(2,128)(2,1)} copy(bf16[8,2,512,384]{3,2,1,0:T(8,128)(2,1)} %all-gather.2.cloned.1.call-done) | data formatting | bytes 12582912 | tf_op jit(solution)/shard_map/while | solution.py:168
  105.8 80.8 %while.26 = (s32[]{:T(128)}, bf16[8,2,64,576]{2,1,3,0:T(2,128)(2,1)}, f32[8,3,3,128,1]{3,2,1,4,0:T(4,128)S(1)}, bf16[8,2,512,384]{2,1,3,0:T(2,128)(2,1)}, s32[2,...) while((s32[]{:T(128)}, ...), condition=%wide.wide.region_5.6_spmd, body=%wide.wide.region_2.5_spmd.sunk | while | flops 316407680 | bytes 21867660 | solution.py:168
  186.6 6.2 copy.79
  203.8 6.3 multiply_convert_fusion
  212.9 3.4 convolution_add_fusion
  216.3 3.2 copy.81
  219.5 4.2 multiply_reduce_fusion
  229.2 335.9 %while.27 = (s32[]{:T(128)}, f32[8,2,64,9,64]{2,4,3,1,0:T(8,128)}, bf16[8,2,512,384]{3,2,1,0:T(8,128)(2,1)}, bf16[8,2,512,384]{2,1,3,0:T(2,128)(2,1)}, s32[2,512...) while((s32[]{:T(128)}, f32[8,2,64,9,64]{2,4,3,1,0:T(8,128)}, ...), condition=%wide.wide.region_10.11_spmd, body=%wide.wide.region_8.10_spmd.sunk | while | flops 786306304 | bytes 50406564 | solution.py:263
  236.4 3.0 fusion.160
  239.5 3.0 fusion.161
  242.5 10.2 %convolution_bitcast_fusion.7 = f32[128,3,3,64]{0,3,2,1:T(8,128)} fusion(f32[3,1024,128,3]{2,1,3,0:T(8,128)} %fusion.160, f32[3,1024,128,3]{2,1,3,0:T(8,128)} %fusion.161, f32[3,3,128]{2,1,0:T(4,128)S(1)} %dynamic-slice_bitcast_fusion.11, pred[128,1024]{0,1:T(8,128)(4,1)S(1)} %compare_and_fusion.7, bf16[1024,3,64,1]{0,2,1,3:T(8,128)(2,1)S(1)} %reshape.310), kind=kOutput, calls=%fused_computation.33.clone.clone.1 | convolution fusion | flops 163973248 | bytes 10260992 | tf_op jit(solution)/shard_map/while/body/eval_jaxpr/cgqk,kcd->qcgd/dot_general | solution.py:116
  252.7 9.5 %convolution_bitcast_fusion.8 = bf16[1024,3,64]{0,2,1:T(8,128)(2,1)S(1)} fusion(bf16[128,3,3,64]{0,3,2,1:T(8,128)(2,1)S(1)} %reshape.309, f32[3,1024,128,3]{2,1,3,0:T(8,128)} %fusion.160, f32[3,1024,128,3]{2,1,3,0:T(8,128)} %fusion.161, f32[3,3,128]{2,1,0:T(4,128)S(1)} %dynamic-slice_bitcast_fusion.11, pred[128,1024]{0,1:T(8,128)(4,1)S(1)} %compare_and_fusion.7), kind=kOutput, calls=%fused_computation.32.clone.clone.1 | convolution fusion | flops 163973248 | bytes 10113536 | tf_op jit(solution)/shard_map/while/body/eval_jaxpr/cgqk,qcgd->kcd/dot_general | solution.py:120
  262.2 3.6 fusion.162
  278.3 3.0 fusion.160
  281.4 3.0 fusion.161
  284.3 10.2 %convolution_bitcast_fusion.7 = f32[128,3,3,64]{0,3,2,1:T(8,128)} fusion(f32[3,1024,128,3]{2,1,3,0:T(8,128)} %fusion.160, f32[3,1024,128,3]{2,1,3,0:T(8,128)} %fusion.161, f32[3,3,128]{2,1,0:T(4,128)S(1)} %dynamic-slice_bitcast_fusion.11, pred[128,1024]{0,1:T(8,128)(4,1)S(1)} %compare_and_fusion.7, bf16[1024,3,64,1]{0,2,1,3:T(8,128)(2,1)S(1)} %reshape.310), kind=kOutput, calls=%fused_computation.33.clone.clone.1 | convolution fusion | flops 163973248 | bytes 10260992 | tf_op jit(solution)/shard_map/while/body/eval_jaxpr/cgqk,kcd->qcgd/dot_general | solution.py:116
  294.5 9.5 %convolution_bitcast_fusion.8 = bf16[1024,3,64]{0,2,1:T(8,128)(2,1)S(1)} fusion(bf16[128,3,3,64]{0,3,2,1:T(8,128)(2,1)S(1)} %reshape.309, f32[3,1024,128,3]{2,1,3,0:T(8,128)} %fusion.160, f32[3,1024,128,3]{2,1,3,0:T(8,128)} %fusion.161, f32[3,3,128]{2,1,0:T(4,128)S(1)} %dynamic-slice_bitcast_fusion.11, pred[128,1024]{0,1:T(8,128)(4,1)S(1)} %compare_and_fusion.7), kind=kOutput, calls=%fused_computation.32.clone.clone.1 | convolution fusion | flops 163973248 | bytes 10113536 | tf_op jit(solution)/shard_map/while/body/eval_jaxpr/cgqk,qcgd->kcd/dot_general | solution.py:120
  304.0 3.6 fusion.162
  320.2 3.0 fusion.160
  323.3 3.0 fusion.161
  326.3 10.2 %convolution_bitcast_fusion.7 = f32[128,3,3,64]{0,3,2,1:T(8,128)} fusion(f32[3,1024,128,3]{2,1,3,0:T(8,128)} %fusion.160, f32[3,1024,128,3]{2,1,3,0:T(8,128)} %fusion.161, f32[3,3,128]{2,1,0:T(4,128)S(1)} %dynamic-slice_bitcast_fusion.11, pred[128,1024]{0,1:T(8,128)(4,1)S(1)} %compare_and_fusion.7, bf16[1024,3,64,1]{0,2,1,3:T(8,128)(2,1)S(1)} %reshape.310), kind=kOutput, calls=%fused_computation.33.clone.clone.1 | convolution fusion | flops 163973248 | bytes 10260992 | tf_op jit(solution)/shard_map/while/body/eval_jaxpr/cgqk,kcd->qcgd/dot_general | solution.py:116
  336.5 9.5 %convolution_bitcast_fusion.8 = bf16[1024,3,64]{0,2,1:T(8,128)(2,1)S(1)} fusion(bf16[128,3,3,64]{0,3,2,1:T(8,128)(2,1)S(1)} %reshape.309, f32[3,1024,128,3]{2,1,3,0:T(8,128)} %fusion.160, f32[3,1024,128,3]{2,1,3,0:T(8,128)} %fusion.161, f32[3,3,128]{2,1,0:T(4,128)S(1)} %dynamic-slice_bitcast_fusion.11, pred[128,1024]{0,1:T(8,128)(4,1)S(1)} %compare_and_fusion.7), kind=kOutput, calls=%fused_computation.32.clone.clone.1 | convolution fusion | flops 163973248 | bytes 10113536 | tf_op jit(solution)/shard_map/while/body/eval_jaxpr/cgqk,qcgd->kcd/dot_general | solution.py:120
  346.0 3.6 fusion.162
  362.2 3.0 fusion.160
  365.2 3.0 fusion.161
  368.2 10.2 %convolution_bitcast_fusion.7 = f32[128,3,3,64]{0,3,2,1:T(8,128)} fusion(f32[3,1024,128,3]{2,1,3,0:T(8,128)} %fusion.160, f32[3,1024,128,3]{2,1,3,0:T(8,128)} %fusion.161, f32[3,3,128]{2,1,0:T(4,128)S(1)} %dynamic-slice_bitcast_fusion.11, pred[128,1024]{0,1:T(8,128)(4,1)S(1)} %compare_and_fusion.7, bf16[1024,3,64,1]{0,2,1,3:T(8,128)(2,1)S(1)} %reshape.310), kind=kOutput, calls=%fused_computation.33.clone.clone.1 | convolution fusion | flops 163973248 | bytes 10260992 | tf_op jit(solution)/shard_map/while/body/eval_jaxpr/cgqk,kcd->qcgd/dot_general | solution.py:116
  378.4 9.5 %convolution_bitcast_fusion.8 = bf16[1024,3,64]{0,2,1:T(8,128)(2,1)S(1)} fusion(bf16[128,3,3,64]{0,3,2,1:T(8,128)(2,1)S(1)} %reshape.309, f32[3,1024,128,3]{2,1,3,0:T(8,128)} %fusion.160, f32[3,1024,128,3]{2,1,3,0:T(8,128)} %fusion.161, f32[3,3,128]{2,1,0:T(4,128)S(1)} %dynamic-slice_bitcast_fusion.11, pred[128,1024]{0,1:T(8,128)(4,1)S(1)} %compare_and_fusion.7), kind=kOutput, calls=%fused_computation.32.clone.clone.1 | convolution fusion | flops 163973248 | bytes 10113536 | tf_op jit(solution)/shard_map/while/body/eval_jaxpr/cgqk,qcgd->kcd/dot_general | solution.py:120
  387.9 3.6 fusion.162
  404.0 3.0 fusion.160
  410.1 10.2 %convolution_bitcast_fusion.7 = f32[128,3,3,64]{0,3,2,1:T(8,128)} fusion(f32[3,1024,128,3]{2,1,3,0:T(8,128)} %fusion.160, f32[3,1024,128,3]{2,1,3,0:T(8,128)} %fusion.161, f32[3,3,128]{2,1,0:T(4,128)S(1)} %dynamic-slice_bitcast_fusion.11, pred[128,1024]{0,1:T(8,128)(4,1)S(1)} %compare_and_fusion.7, bf16[1024,3,64,1]{0,2,1,3:T(8,128)(2,1)S(1)} %reshape.310), kind=kOutput, calls=%fused_computation.33.clone.clone.1 | convolution fusion | flops 163973248 | bytes 10260992 | tf_op jit(solution)/shard_map/while/body/eval_jaxpr/cgqk,kcd->qcgd/dot_general | solution.py:116
  420.3 9.5 %convolution_bitcast_fusion.8 = bf16[1024,3,64]{0,2,1:T(8,128)(2,1)S(1)} fusion(bf16[128,3,3,64]{0,3,2,1:T(8,128)(2,1)S(1)} %reshape.309, f32[3,1024,128,3]{2,1,3,0:T(8,128)} %fusion.160, f32[3,1024,128,3]{2,1,3,0:T(8,128)} %fusion.161, f32[3,3,128]{2,1,0:T(4,128)S(1)} %dynamic-slice_bitcast_fusion.11, pred[128,1024]{0,1:T(8,128)(4,1)S(1)} %compare_and_fusion.7), kind=kOutput, calls=%fused_computation.32.clone.clone.1 | convolution fusion | flops 163973248 | bytes 10113536 | tf_op jit(solution)/shard_map/while/body/eval_jaxpr/cgqk,qcgd->kcd/dot_general | solution.py:120
  429.8 3.6 fusion.162
  446.0 3.0 fusion.160
  449.0 3.0 fusion.161
  452.0 10.2 %convolution_bitcast_fusion.7 = f32[128,3,3,64]{0,3,2,1:T(8,128)} fusion(f32[3,1024,128,3]{2,1,3,0:T(8,128)} %fusion.160, f32[3,1024,128,3]{2,1,3,0:T(8,128)} %fusion.161, f32[3,3,128]{2,1,0:T(4,128)S(1)} %dynamic-slice_bitcast_fusion.11, pred[128,1024]{0,1:T(8,128)(4,1)S(1)} %compare_and_fusion.7, bf16[1024,3,64,1]{0,2,1,3:T(8,128)(2,1)S(1)} %reshape.310), kind=kOutput, calls=%fused_computation.33.clone.clone.1 | convolution fusion | flops 163973248 | bytes 10260992 | tf_op jit(solution)/shard_map/while/body/eval_jaxpr/cgqk,kcd->qcgd/dot_general | solution.py:116
  462.2 9.5 %convolution_bitcast_fusion.8 = bf16[1024,3,64]{0,2,1:T(8,128)(2,1)S(1)} fusion(bf16[128,3,3,64]{0,3,2,1:T(8,128)(2,1)S(1)} %reshape.309, f32[3,1024,128,3]{2,1,3,0:T(8,128)} %fusion.160, f32[3,1024,128,3]{2,1,3,0:T(8,128)} %fusion.161, f32[3,3,128]{2,1,0:T(4,128)S(1)} %dynamic-slice_bitcast_fusion.11, pred[128,1024]{0,1:T(8,128)(4,1)S(1)} %compare_and_fusion.7), kind=kOutput, calls=%fused_computation.32.clone.clone.1 | convolution fusion | flops 163973248 | bytes 10113536 | tf_op jit(solution)/shard_map/while/body/eval_jaxpr/cgqk,qcgd->kcd/dot_general | solution.py:120
  471.7 3.6 fusion.162
  487.8 3.0 fusion.160
  490.9 3.0 fusion.161
  493.9 10.2 %convolution_bitcast_fusion.7 = f32[128,3,3,64]{0,3,2,1:T(8,128)} fusion(f32[3,1024,128,3]{2,1,3,0:T(8,128)} %fusion.160, f32[3,1024,128,3]{2,1,3,0:T(8,128)} %fusion.161, f32[3,3,128]{2,1,0:T(4,128)S(1)} %dynamic-slice_bitcast_fusion.11, pred[128,1024]{0,1:T(8,128)(4,1)S(1)} %compare_and_fusion.7, bf16[1024,3,64,1]{0,2,1,3:T(8,128)(2,1)S(1)} %reshape.310), kind=kOutput, calls=%fused_computation.33.clone.clone.1 | convolution fusion | flops 163973248 | bytes 10260992 | tf_op jit(solution)/shard_map/while/body/eval_jaxpr/cgqk,kcd->qcgd/dot_general | solution.py:116
  504.1 9.5 %convolution_bitcast_fusion.8 = bf16[1024,3,64]{0,2,1:T(8,128)(2,1)S(1)} fusion(bf16[128,3,3,64]{0,3,2,1:T(8,128)(2,1)S(1)} %reshape.309, f32[3,1024,128,3]{2,1,3,0:T(8,128)} %fusion.160, f32[3,1024,128,3]{2,1,3,0:T(8,128)} %fusion.161, f32[3,3,128]{2,1,0:T(4,128)S(1)} %dynamic-slice_bitcast_fusion.11, pred[128,1024]{0,1:T(8,128)(4,1)S(1)} %compare_and_fusion.7), kind=kOutput, calls=%fused_computation.32.clone.clone.1 | convolution fusion | flops 163973248 | bytes 10113536 | tf_op jit(solution)/shard_map/while/body/eval_jaxpr/cgqk,qcgd->kcd/dot_general | solution.py:120
  513.6 3.6 fusion.162
  529.8 3.0 fusion.160
  532.8 3.0 fusion.161
  535.8 10.2 %convolution_bitcast_fusion.7 = f32[128,3,3,64]{0,3,2,1:T(8,128)} fusion(f32[3,1024,128,3]{2,1,3,0:T(8,128)} %fusion.160, f32[3,1024,128,3]{2,1,3,0:T(8,128)} %fusion.161, f32[3,3,128]{2,1,0:T(4,128)S(1)} %dynamic-slice_bitcast_fusion.11, pred[128,1024]{0,1:T(8,128)(4,1)S(1)} %compare_and_fusion.7, bf16[1024,3,64,1]{0,2,1,3:T(8,128)(2,1)S(1)} %reshape.310), kind=kOutput, calls=%fused_computation.33.clone.clone.1 | convolution fusion | flops 163973248 | bytes 10260992 | tf_op jit(solution)/shard_map/while/body/eval_jaxpr/cgqk,kcd->qcgd/dot_general | solution.py:116
  546.0 9.5 %convolution_bitcast_fusion.8 = bf16[1024,3,64]{0,2,1:T(8,128)(2,1)S(1)} fusion(bf16[128,3,3,64]{0,3,2,1:T(8,128)(2,1)S(1)} %reshape.309, f32[3,1024,128,3]{2,1,3,0:T(8,128)} %fusion.160, f32[3,1024,128,3]{2,1,3,0:T(8,128)} %fusion.161, f32[3,3,128]{2,1,0:T(4,128)S(1)} %dynamic-slice_bitcast_fusion.11, pred[128,1024]{0,1:T(8,128)(4,1)S(1)} %compare_and_fusion.7), kind=kOutput, calls=%fused_computation.32.clone.clone.1 | convolution fusion | flops 163973248 | bytes 10113536 | tf_op jit(solution)/shard_map/while/body/eval_jaxpr/cgqk,qcgd->kcd/dot_general | solution.py:120
  555.5 3.6 fusion.162
  565.9 3.1 multiply_add_fusion
  569.7 3.9 copy.88
  573.5 6.5 convert_element_type.156
  580.1 3.5 convolution_convert_fusion.4
  586.2 3.3 convolution_convert_fusion.1
  589.5 3.3 convolution_convert_fusion.2
  592.8 3.3 convolution_convert_fusion
  596.1 37.7 %reduce-scatter.2.cloned.1.call-done = bf16[8,2,64,384]{3,2,1,0:T(8,128)(2,1)} async-done(((bf16[8,2,512,384]{3,2,1,0:T(8,128)(2,1)}), bf16[8,2,64,384]{3,2,1,0:T(8,128)(2,1)}) %reduce-scatter.2.cloned.1.call-update) | async-done | bytes 786448 | tf_op jit(solution)/shard_map/reduce_scatter | solution.py:267
  649.4 6.0 fusion.62
  659.7 3.3 copy.92
  663.0 3.6 fusion.48
  666.6 39.3 %all-reduce = (f32[576]{0:T(1024)}, f32[576]{0:T(1024)}) all-reduce(f32[576]{0:T(1024)S(1)} %get-tuple-element.167, f32[576]{0:T(1024)S(1)} %get-tuple-element.165), channel_id=1, replica_groups=mesh['seq'=8,'batch'=4] {'seq','batch'}, use_global_device_ids=true, to_apply=%region_14.15 | all-reduce | flops 1152 | bytes 9216 | tf_op jit(solution)/shard_map/psum | solution.py:294
  705.9 6.7 fusion.45
  712.6 106.4 %all-reduce.4.cloned.1.call-done = (bf16[576,576]{1,0:T(8,128)(2,1)}, bf16[576,192]{0,1:T(8,128)(2,1)}, bf16[576,192]{0,1:T(8,128)(2,1)}, bf16[576,576]{1,0:T(8,...) async-done(((bf16[576,576]{1,0:T(8,128)(2,1)}, bf16[576,192]{0,1:T(8,128)(2,1)}, bf16[576,192]{0,1:T(8,128)(2,1)}, ...) | async-done | bytes 7077904 | tf_op jit(solution)/shard_map/psum | solution.py:290
  (461 shorter events, 259.8 us)
Async XLA Ops:
  7.2 196.6 %copy-start = (bf16[1536,576]{0,1:T(8,128)(2,1)S(1)}, bf16[1536,576]{0,1:T(8,128)(2,1)}, u32[]{:S(2)}) copy-start(bf16[1536,576]{0,1:T(8,128)(2,1)} %param.28) | copy-start | bytes 5308420
  7.2 82.1 %all-gather.2.cloned.1.call-start = ((), (), s32[]{:S(2)}) async-start(), calls=%async_computation.1 | async-start | bytes 7077888 | tf_op jit(solution)/shard_map/all_gather | solution.py:227
  7.3 4.9 copy-start.24
  8.1 4.0 copy-start.33
  10.4 1.7 copy-start.31
  12.1 12.1 %copy-start.6 = (bf16[8,2,64,576]{3,2,1,0:T(8,128)(2,1)}, bf16[8,2,64,576]{3,2,1,0:T(8,128)(2,1)S(1)}, u32[]{:S(2)}) copy-start(bf16[8,2,64,576]{3,2,1,0:T(8,128)(2,1)S(1)} %fusion.42) | copy-start | bytes 3538948
  15.5 17.4 %copy-start.36 = (s32[2,64]{1,0:T(2,128)}, s32[2,64]{1,0:T(2,128)S(1)}, u32[]{:S(2)}) copy-start(s32[2,64]{1,0:T(2,128)S(1)} %get-tuple-element.494) | copy-start | bytes 1540
  15.7 11.7 %copy-start.26 = (f32[2,64,32]{1,2,0:T(8,128)}, f32[2,64,32]{1,2,0:T(8,128)S(1)}, u32[]{:S(2)}) copy-start(f32[2,64,32]{1,2,0:T(8,128)S(1)} %get-tuple-element.239) | copy-start | bytes 49156
  15.7 11.7 %copy-start.28 = (f32[2,64,32]{1,2,0:T(8,128)}, f32[2,64,32]{1,2,0:T(8,128)S(1)}, u32[]{:S(2)}) copy-start(f32[2,64,32]{1,2,0:T(8,128)S(1)} %get-tuple-element.240) | copy-start | bytes 49156
  16.0 6.0 copy-start.37
  21.8 612.0 %reduce-scatter.2.cloned.1.call-start = ((), (), s32[]{:S(2)}) async-start(), calls=%async_computation.2 | async-start | bytes 7077888 | tf_op jit(solution)/shard_map/reduce_scatter | solution.py:267
  28.7 4.0 copy-start.41
  28.7 4.0 copy-start.42
  28.8 4.2 copy-start.8
  186.6 6.2 copy-start.4
  195.7 5.4 copy-start.2
  195.8 2.8 copy-start.39
  196.1 5.1 copy-start.19
  198.6 2.6 copy-start.38
  201.2 2.6 copy-start.17
  210.2 2.0 copy-start.43
  210.2 2.7 copy-start.45
  219.4 4.2 copy-start.1
  219.4 4.8 copy-start.3
  219.4 5.2 copy-start.9
  224.6 2.1 copy-start.40
  225.6 1.1 copy-start.21
  565.1 0.8 copy-start.27
  565.1 0.8 copy-start.29
  565.2 253.9 %all-reduce.4.cloned.1.call-start = ((), (), s32[]{:S(2)}) async-start(), calls=%async_computation.3 | async-start | bytes 14548992 | tf_op jit(solution)/shard_map/psum | solution.py:290
  573.5 6.5 copy-start.7
  580.1 3.5 copy-start.16
  580.1 3.5 copy-start.22
  583.6 2.0 copy-start.20
  583.6 2.6 copy-start.46
  586.2 3.3 copy-start.44
  589.5 3.3 copy-start.18
  589.5 3.3 copy-start.47
  649.4 6.1 copy-start.23
  655.5 1.0 copy-start.12
  655.5 1.1 copy-start.25
  655.5 1.6 copy-start.10
  655.5 1.7 copy-start.11
  659.7 3.3 copy-start.5
  659.7 3.3 copy-start.32
  659.7 3.3 copy-start.34
  663.0 42.9 %copy-start.35 = (f32[8,2,64]{2,1,0:T(2,128)S(1)}, f32[8,2,64]{2,1,0:T(2,128)}, u32[]{:S(2)}) copy-start(f32[8,2,64]{2,1,0:T(2,128)} %get-tuple-element.235) | copy-start | bytes 12292
  819.0 6.0 copy-start.30
  820.9 5.4 copy-start.15
  826.3 2.3 copy-start.14
  828.6 2.3 copy-start.13
Sparse Core Ops, SparseCore 0:
  21.9 67.4 all-gather.1
  565.3 68.4 reduce-scatter.1
  649.5 169.4 all-reduce.3
